TPU v7x, 128 devices: a whole 4x4x4 slice. The times are simulated.
128 devices in a mesh: seq: 32 (over z, x, core), head: 4 (over y).
Axes of the slice: x: 4, y: 4, z: 4, core: 2. Of those that a mesh axis runs over, the one named last changes fastest.
Arguments:
- values_in: bfloat16 [16384, 16384], P(('seq', 'head')), may hold values from -6 to 6
- factors_in: bfloat16 [16384, 8, 2, 256], P(('seq', 'head')), may hold values from -6 to 6
- step_raw: bfloat16 [16384, 256], P(('seq', 'head')), may hold values from -16 to 0
- gate_in: bfloat16 [16384, 16384], P(('seq', 'head')), may hold values from -100 to 100
- conv_values: bfloat16 [4, 16384], replicated, may hold values from -3 to 3
- conv_factors: bfloat16 [4, 8, 2, 256], replicated, may hold values from -3 to 3
- decay_log: float32 [256], replicated, may hold values from -0.3 to 0.3
- skip_gain: float32 [256], replicated, may hold values from 0.5 to 1.5
- norm_gain: float32 [16384], replicated, may hold values from 0.5 to 1.5
Outputs:
- mixed_out: bfloat16 [16384, 16384], P(('seq', 'head'))
All inputs are finite; a program needn't handle non-finite values.
Results may differ from a plain program's by a relative error of at most 0.0055.
Values may be sent and summed in bfloat16 or wider, within the bound.
A program may use at most 448 MiB of HBM per device.

v0:
```python
from functools import partial

import jax
import jax.numpy as jnp
from jax import lax
from jax.sharding import PartitionSpec as P

SCAN_HEADS = 256
HEAD_DIM = 64
STATE = 256
GROUPS = 8
SPAN = 128
CONV = 4


def from_behind(value, axis, by):
    size = lax.axis_size(axis)
    pairs = [(i, i + by) for i in range(size) if 0 <= i + by < size]
    return lax.ppermute(value, axis, pairs)


def prefix(value, axis, join, neutral):
    count, mine = (lax.axis_size(axis), lax.axis_index(axis))
    pieces = jax.tree.map(lambda part: lax.all_gather(part, axis), value)
    subtotal = jax.tree.map(
        lambda part, zero: jnp.full_like(part, 0) + jnp.asarray(zero, part.dtype), value, neutral
    )

    def hop(position, subtotal):
        longer = join(subtotal, jax.tree.map(lambda part: part[position], pieces))
        return jax.tree.map(lambda new, old: jnp.where(position < mine, new, old), longer, subtotal)

    return lax.fori_loop(0, count - 1, hop, subtotal)


def convolve(current, before_rows, weight):
    tap_count = weight.shape[0]
    row_count = current.shape[0]
    padded = jnp.concatenate([before_rows, current], axis=0)
    summed = jnp.zeros(current.shape, jnp.float32)
    for offset in range(tap_count):
        summed = summed + padded[offset : offset + row_count].astype(jnp.float32) * weight[
            offset
        ].astype(jnp.float32)
    return jax.nn.silu(summed).astype(jnp.bfloat16)


def block_terms(decay_rate, state_in, blocks):
    signal, b_factor, c_factor, step_sizes = blocks
    row_count = signal.shape[0]
    running = jnp.cumsum(-step_sizes * decay_rate, axis=0)
    scores = jnp.einsum("tgn,sgn->gts", c_factor, b_factor, preferred_element_type=jnp.float32)
    causal = jnp.arange(row_count)[:, None] >= jnp.arange(row_count)[None, :]
    running_heads = jnp.transpose(running, (1, 2, 0))
    spacing = jnp.where(causal, running_heads[..., :, None] - running_heads[..., None, :], 0.0)
    step_heads = jnp.transpose(step_sizes, (1, 2, 0))
    mixing = jnp.where(
        causal, jnp.exp(spacing) * step_heads[..., None, :] * scores[:, None], 0.0
    ).astype(jnp.bfloat16)
    within = jnp.einsum("gjts,sgjp->tgjp", mixing, signal, preferred_element_type=jnp.float32)
    weights_end = jnp.exp(running[-1] - running) * step_sizes
    weighted = (weights_end[..., None] * signal.astype(jnp.float32)).astype(jnp.bfloat16)
    fresh_state = jnp.einsum(
        "sgjp,sgn->gjpn", weighted, b_factor, preferred_element_type=jnp.float32
    )
    new_state = jnp.exp(running[-1])[..., None, None] * state_in + fresh_state
    return (new_state, (within, state_in, running))


def gated_norm(outputs, gate_values, gain_row, norm_parts):
    row_total = outputs.shape[0]
    gated_values = outputs.astype(jnp.float32) * jax.nn.silu(gate_values.astype(jnp.float32))
    grouped = gated_values.reshape(row_total, norm_parts, -1)
    inverse_rms = lax.rsqrt(jnp.mean(grouped * grouped, axis=-1, keepdims=True) + 1e-05)
    return ((grouped * inverse_rms).reshape(row_total, -1) * gain_row).astype(jnp.bfloat16)


def combine(earlier_part, later_part):
    return (
        earlier_part[0] * later_part[0],
        later_part[0][..., None, None] * earlier_part[1] + later_part[1],
    )


def local(
    values_in,
    factors_in,
    step_raw,
    gate_in,
    conv_values,
    conv_factors,
    decay_log,
    skip_gain,
    norm_gain,
):
    row_count = values_in.shape[0]
    head_parts = lax.axis_size("head")
    local_heads = SCAN_HEADS // head_parts
    local_groups = GROUPS // head_parts
    per_group = SCAN_HEADS // GROUPS
    head_index = lax.axis_index("head")
    margin = CONV - 1
    values_heads = values_in.reshape(row_count, SCAN_HEADS, HEAD_DIM)
    conv_heads = conv_values.reshape(CONV, SCAN_HEADS, HEAD_DIM)
    before_values, before_factors = from_behind(
        (values_heads[row_count - margin :], factors_in[row_count - margin :]), ("seq", "head"), 1
    )
    signal_rows = convolve(values_heads, before_values, conv_heads)
    factor_rows = convolve(factors_in, before_factors, conv_factors)
    signal_h, factor_h, step_h = (
        lax.all_to_all(signal_rows, "head", split_axis=1, concat_axis=0, tiled=True),
        lax.all_to_all(factor_rows, "head", split_axis=1, concat_axis=0, tiled=True),
        lax.all_to_all(step_raw, "head", split_axis=1, concat_axis=0, tiled=True),
    )
    total_rows = signal_h.shape[0]
    blocks = total_rows // SPAN
    decay_rate = jnp.exp(
        lax.dynamic_slice_in_dim(decay_log, head_index * local_heads, local_heads, 0)
    ).reshape(local_groups, per_group)
    skip_local = lax.dynamic_slice_in_dim(
        skip_gain, head_index * local_heads, local_heads, 0
    ).reshape(local_groups, per_group)
    step_sizes = jax.nn.softplus(step_h.astype(jnp.float32)).reshape(
        blocks, SPAN, local_groups, per_group
    )
    signal_blocks = signal_h.reshape(blocks, SPAN, local_groups, per_group, HEAD_DIM)
    b_factor = factor_h[:, :, 0].reshape(blocks, SPAN, local_groups, STATE)
    c_factor = factor_h[:, :, 1].reshape(blocks, SPAN, local_groups, STATE)
    empty_state = jnp.zeros((local_groups, per_group, HEAD_DIM, STATE), jnp.float32)
    end_state, (within, local_entry, running) = lax.scan(
        partial(block_terms, decay_rate),
        empty_state,
        (signal_blocks, b_factor, c_factor, step_sizes),
    )
    block_totals = running[:, -1]
    prior_log = jnp.cumsum(block_totals, axis=0) - block_totals
    device_decay = jnp.exp(jnp.sum(block_totals, axis=0))
    identity = (jnp.ones_like(device_decay), jnp.zeros_like(end_state))
    entry_decay, state_before = prefix((device_decay, end_state), "seq", combine, identity)
    entering = local_entry + jnp.exp(prior_log)[..., None, None] * state_before[None]
    from_state = jnp.einsum(
        "ktgn,kgjpn->ktgjp",
        c_factor,
        entering.astype(jnp.bfloat16),
        preferred_element_type=jnp.float32,
    )
    result = (
        within
        + jnp.exp(running)[..., None] * from_state
        + skip_local[..., None] * signal_blocks.astype(jnp.float32)
    )
    ssm_out = result.astype(jnp.bfloat16).reshape(total_rows, local_heads, HEAD_DIM)
    back_rows = lax.all_to_all(ssm_out, "head", split_axis=0, concat_axis=1, tiled=True)
    mixed_out = gated_norm(
        back_rows.reshape(row_count, SCAN_HEADS * HEAD_DIM), gate_in, norm_gain, GROUPS
    )
    return mixed_out


def solution(mesh):
    placed = (
        P(("seq", "head"), None),
        P(("seq", "head"), None, None, None),
        P(("seq", "head"), None),
        P(("seq", "head"), None),
        P(),
        P(),
        P(),
        P(),
        P(),
    )
    return jax.shard_map(
        local, mesh=mesh, in_specs=placed, out_specs=P(("seq", "head"), None), check_vma=False
    )
```

profile of v0, /device:TPU:0, one launch (start us, length us, event | category | flops | bytes accessed | tf_op | source)
XLA Modules:
  0.0 876.9 jit_solution(5776572328138287095)
XLA Ops:
  24.0 6.4 copy.84
  41.3 19.9 %multiply_convert_fusion.2 = bf16[128,256,64]{0,2,1:T(8,128)(2,1)} fusion(bf16[128,256,64]{0,2,1:T(8,128)(2,1)} %bitcast.150, bf16[3,256,64]{0,2,1:T(8,128)(2,1)} %copy.85, f32[256,64]{1,0:T(8,128)S(1)} %reshape.125, f32[256,64]{1,0:T(8,128)S(1)} %reshape.124, f32[256,64]{1,0:T(8,128)S(1)} %reshape.123, f32[256,64]{1,0:T(8,128)S(1)} %reshape.122), kind=kLoop, calls=%fused_computation.63 | loop fusion | flops 52428800 | bytes 8749056 | tf_op jit(solution)/shard_map/convert_element_type | solution.py:45
  66.6 48.7 %all-to-all-done.1 = bf16[128,256,64]{0,2,1:T(8,128)(2,1)} async-done(((bf16[128,256,64]{0,2,1:T(8,128)(2,1)}), bf16[128,256,64]{0,2,1:T(8,128)(2,1)}, u32[]{:S(2)}, u32[]{:S(2)}) %all-to-all-start.1) | async-done | bytes 4194336 | tf_op jit(solution)/shard_map/all_to_all | solution.py:111
  115.4 55.6 %while.31 = (s32[]{:T(128)}, f32[2,32,64,256]{3,2,1,0:T(8,128)}, f32[4,128,2,32,64]{1,4,3,2,0:T(8,128)}, f32[4,2,32,64,256]{4,3,2,1,0:T(8,128)}, f32[4,128,2,32]...) while((s32[]{:T(128)}, f32[2,32,64,256]{3,2,1,0:T(8,128)}, ...), condition=%wide.region_2.3_spmd.clone, body=%wide.region_0.2_spmd.clone.sunk | while | flops 432578560 | bytes 22617480 | solution.py:130
  172.3 25.4 %all-gather.2 = f32[32,2,32]{2,1,0:T(2,128)S(1)} all-gather(f32[1,2,32]{2,1,0:T(2,128)S(1)} %exponential_bitcast_fusion), channel_id=2, replica_groups=mesh['seq'=32,'head'=4] {'seq'}, dimensions={0}, use_global_device_ids=true | all-gather | bytes 8448 | tf_op jit(solution)/shard_map/all_gather | solution.py:24
  197.7 349.3 %all-gather.5.cloned.1.call-done = f32[64,32,64,256]{3,2,1,0:T(8,128)} async-done(((f32[2,32,64,256]{3,2,1,0:T(8,128)}), f32[64,32,64,256]{3,2,1,0:T(8,128)}) %all-gather.5.cloned.1.call-update) | async-done | bytes 134217744 | tf_op jit(solution)/shard_map/all_gather | solution.py:24
  547.0 185.1 %while.32 = (s32[]{:T(128)}, f32[2,32,64,256]{3,2,1,0:T(8,128)}, s32[]{:T(128)}, f32[32,2,32]{2,1,0:T(2,128)S(1)}, f32[32,2,32,64,256]{4,3,2,1,0:T(8,128)}, /*index=5*/s32[]{:T(128)}, s32[]{:T(128)}) while((s32[]{:T(128)}, f32[2,32,64,256]{3,2,1,0:T(8,128)}, s32[]{:T(128)}, f32[32,2,32]{2,1,0:T(2,128)S(1)}, ...), condition=%wide.region_6.7_spmd.clone, body=%wide.region_5.6_spmd.clone.sunk | while | flops 4194308 | bytes 12583785 | solution.py:33
  551.7 6.0 fusion.63
  557.7 6.0 fusion.63
  563.7 6.0 fusion.63
  569.7 6.0 fusion.63
  575.8 6.0 fusion.63
  581.8 6.0 fusion.63
  587.8 6.0 fusion.63
  593.8 6.0 fusion.63
  732.1 14.3 %fusion.38 = bf16[4,128,2,32,64]{1,4,3,2,0:T(8,128)(2,1)} fusion(f32[4,128,2,32,64]{1,4,3,2,0:T(8,128)} %get-tuple-element.154, bf16[4,128,2,32,64]{1,4,3,2,0:T(8,128)(2,1)} %bitcast.7, f32[2,32]{1,0:T(2,128)S(1)} %mul.264, f32[4,128,2,32]{1,3,2,0:T(8,128)S(1)} %copy.94, f32[4,2,32,64,256]{4,3,2,1,0:T(8,128)} %get-tuple-element.156, ...), kind=kOutput, calls=%fused_computation.60 | convolution fusion | flops 1098907648 | bytes 38405376 | tf_op jit(solution)/shard_map/ktgn,kgjpn->ktgjp/dot_general | solution.py:141
  746.4 13.0 %copy.106 = bf16[4,128,2,32,64]{4,3,2,1,0:T(8,128)(2,1)} copy(bf16[4,128,2,32,64]{1,4,3,2,0:T(8,128)(2,1)} %fusion.38) | data formatting | bytes 8388608 | tf_op jit(solution)/shard_map/reshape | solution.py:152
  759.4 9.5 %reshape.161 = bf16[4,2,262144]{2,1,0:T(2,128)(2,1)} reshape(bf16[512,64,64]{2,1,0:T(8,128)(2,1)} %bitcast.147) | data formatting | bytes 8388608
  773.8 6.4 copy.100
  780.2 43.2 %all-to-all-done.3 = bf16[4,2,262144]{2,1,0:T(2,128)(2,1)} async-done(((bf16[4,2,262144]{2,1,0:T(2,128)(2,1)}), bf16[4,2,262144]{2,1,0:T(2,128)(2,1)}, u32[]{:S(2)}, u32[]{:S(2)}) %all-to-all-start.3) | async-done | bytes 4194336 | tf_op jit(solution)/shard_map/all_to_all | solution.py:153
  823.4 9.3 %reshape.162 = bf16[512,64,64]{2,1,0:T(8,128)(2,1)} reshape(bf16[4,2,262144]{2,1,0:T(2,128)(2,1)} %all-to-all-done.3) | data formatting | bytes 8388608
  832.7 9.7 %copy.98 = bf16[512,64,64]{0,2,1:T(8,128)(2,1)} copy(bf16[512,64,64]{2,1,0:T(8,128)(2,1)} %reshape.162) | data formatting | bytes 8388608 | tf_op jit(solution)/shard_map/all_to_all | solution.py:153
  842.4 8.3 reshape.131
  863.7 6.4 copy.101
  (168 shorter events, 245.4 us)
Async XLA Ops:
  8.1 22.6 %collective-permute-start.1 = (bf16[3,8,2,256]{3,0,2,1:T(4,128)(2,1)S(1)}, bf16[3,8,2,256]{3,0,2,1:T(4,128)(2,1)S(1)}, u32[]{:S(2)}, u32[]{:S(2)}) collective-permute-start(bf16[3,8,2,256]{3,0,2,1:T(4,128)(2,1)S(1)} %slice.94), channel_id=1, source_target_pairs={{0,1},{1,2},{2,3},{3,4},{4,5},{5,6},{6,7},{7,8},{8,9},{9,10},{10,1... | collective-permute-start | bytes 73736 | tf_op jit(solution)/shard_map/ppermute | solution.py:19
  12.9 20.2 %collective-permute-start = (bf16[3,256,64]{2,1,0:T(8,128)(2,1)S(1)}, bf16[3,256,64]{2,1,0:T(8,128)(2,1)S(1)}, u32[]{:S(2)}, u32[]{:S(2)}) collective-permute-start(bf16[3,256,64]{2,1,0:T(8,128)(2,1)S(1)} %slice.69), channel_id=1, source_target_pairs={{0,1},{1,2},{2,3},{3,4},{4,5},{5,6},{6,7},{7,8},{8,9},{9,10},{10,1... | collective-permute-start | bytes 294920 | tf_op jit(solution)/shard_map/ppermute | solution.py:19
  18.0 18.6 %all-to-all-start = ((bf16[128,4,64]{0,2,1:T(8,128)(2,1)}), bf16[128,4,64]{0,2,1:T(8,128)(2,1)S(1)}, u32[]{:S(2)}, u32[]{:S(2)}) async-start(bf16[128,4,64]{0,2,1:T(8,128)(2,1)} %bitcast), calls=%async_computation | async-start | bytes 131072 | tf_op jit(solution)/shard_map/all_to_all | solution.py:113
  36.6 24.6 %all-to-all-start.2 = ((bf16[128,8,2,256]{3,0,2,1:T(8,128)(2,1)}), bf16[128,8,2,256]{3,0,2,1:T(8,128)(2,1)S(1)}, u32[]{:S(2)}, u32[]{:S(2)}) async-start(bf16[128,8,2,256]{3,0,2,1:T(8,128)(2,1)} %multiply_convert_fusion.3), calls=%async_computation.2 | async-start | bytes 2097152 | tf_op jit(solution)/shard_map/all_to_all | solution.py:112
  61.2 5.1 copy-start.2
  61.2 54.1 %all-to-all-start.1 = ((bf16[128,256,64]{0,2,1:T(8,128)(2,1)}), bf16[128,256,64]{0,2,1:T(8,128)(2,1)}, u32[]{:S(2)}, u32[]{:S(2)}) async-start(bf16[128,256,64]{0,2,1:T(8,128)(2,1)} %multiply_convert_fusion.2), calls=%async_computation.1 | async-start | bytes 8388608 | tf_op jit(solution)/shard_map/all_to_all | solution.py:111
  66.2 480.8 %all-gather.5.cloned.1.call-start = ((), (), s32[]{:S(2)}) async-start(), calls=%async_computation.4 | async-start | bytes 138412032 | tf_op jit(solution)/shard_map/all_gather | solution.py:24
  171.0 0.7 copy-start.3
  768.9 54.5 %all-to-all-start.3 = ((bf16[4,2,262144]{2,1,0:T(2,128)(2,1)}), bf16[4,2,262144]{2,1,0:T(2,128)(2,1)}, u32[]{:S(2)}, u32[]{:S(2)}) async-start(bf16[4,2,262144]{2,1,0:T(2,128)(2,1)} %reshape.161), calls=%async_computation.3 | async-start | bytes 8388608 | tf_op jit(solution)/shard_map/all_to_all | solution.py:153
  850.7 4.7 copy-start
  855.5 3.4 copy-start.1
Sparse Core Ops, SparseCore 0:
  171.1 375.7 all-gather.4
where the time goes:
time: 879 us; the launch traced here: 877 us
  waiting for transfers between devices  441 us (50%)
  other arithmetic  236 us (27%)
  local copies, waits for them, and re-layouts  85 us (10%)
  matrix products  50.3 us (6%)
  blocking collectives  25.4 us (3%)
  starting transfers between devices  25 us (3%)
  between operations  13.7 us (2%)
    all_gather x1, waiting for transfers between devices, prefix(): pieces = jax.tree.map(lambda part: lax.all_gather(part, axis), value)  349 us
    select_n x31, other arithmetic, hop(): jnp.where(position < mine, new, old)  185 us
    all_to_all x1, waiting for transfers between devices, local(): lax.all_to_all(signal_rows, 'head', split_axis=1, concat_axis=0, tiled=True)  48.7 us
    all_to_all x1, waiting for transfers between devices, local(): lax.all_to_all(ssm_out, 'head', split_axis=0, concat_axis=1, tiled=True)  43.2 us
    unnamed x15, local copies, waits for them, and re-layouts  35.3 us
    all_gather x1, blocking collectives, prefix(): pieces = jax.tree.map(lambda part: lax.all_gather(part, axis), value)  25.4 us
    convert_element_type x2, other arithmetic, convolve(): return jax.nn.silu(summed).astype(jnp.bfloat16)  22.2 us
    dot_general x4, matrix products, block_terms(): jnp.einsum('sgjp,sgn->gjpn', weighted, b_factor, preferred_element_type=j...  19.7 us
  transfers between devices with their start and end apart: 7, of which 3 were waited for; matrix products, arithmetic and copies ran while one was open for 5% of the time, Pallas kernels for 0%

commit v1 on v0

v1 whole, which is shorter than its diff:
```python
from functools import partial

import jax
import jax.numpy as jnp
from jax import lax
from jax.experimental import pallas as pl
from jax.experimental.pallas import tpu as pltpu
from jax.sharding import PartitionSpec as P

HEAD_DIM = 64
STATE = 256
GROUPS = 8
SPAN = 128
CONV = 4
CHUNKS = 4
AHEAD = 2
LANES = 256
F32 = jnp.float32
BF16 = jnp.bfloat16
MESH = pl.DeviceIdType.MESH


def silu(value):
    return value * pl.reciprocal(1.0 + jnp.exp(-value))


def silu_wide(value):
    inner = value * pl.reciprocal(1.0 + jnp.exp(jnp.minimum(-value, 87.0)))
    return jnp.where(value < -87.0, 0.0, inner)


def softplus_below_zero(value):
    e = jnp.exp(value)
    z = e / (2.0 + e)
    q = z * z
    series = 1.0 / 15.0
    for odd in (13.0, 11.0, 9.0, 7.0, 5.0, 3.0, 1.0):
        series = series * q + 1.0 / odd
    return 2.0 * z * series


def split_columns(rows):
    heads = rows.shape[0]
    high = rows.astype(BF16).astype(F32)
    middle = (rows - high).astype(BF16).astype(F32)
    low = rows - high - middle
    parts = [high, middle, low]
    if 128 > 3 * heads:
        parts.append(jnp.zeros((128 - 3 * heads, rows.shape[1]), F32))
    return jnp.transpose(jnp.concatenate(parts, axis=0)).astype(BF16)


def convolved(current, before, taps):
    padded = jnp.concatenate([before, current], axis=0)
    total = padded[5 : 5 + SPAN] * taps[0:1]
    for offset in range(1, CONV):
        total = total + padded[5 + offset : 5 + offset + SPAN] * taps[offset : offset + 1]
    return silu(total).astype(BF16)


def body(
    values_hbm, gate_hbm, fac_in, step_in, halo_in, conv_v, conv_f, decay, skip, gain,
    out_hbm,
    vals, gate, halo_rx, halo_v, halo_f,
    sig_send, sig_recv, fac_send, fac_recv, stp_recv,
    step_t, run_t, run_c, w_s, t_s, g_s, b_t, scores, expander,
    state, local_entry, s_send, st_recv, e_send, e_recv, d_recv, d_wide,
    part, weighted, gated, squares, y_recv,
    val_sem, gate_sem, out_sem, halo_sem,
    sig_ss, sig_rs, fac_ss, fac_rs, stp_ss, stp_rs, d_ss, d_rs,
    st_ss, st_rs, e_ss, e_rs, y_ss, y_rs,
    *, heads, supers,
):
    channels = heads * HEAD_DIM
    width = channels // CHUNKS
    chunk_heads = heads // CHUNKS
    slice_rows = STATE // supers
    lanes = min(LANES, width)

    seq, col = lax.axis_index("seq"), lax.axis_index("head")
    core = lax.rem(seq, 2)
    mine = seq // 2
    me = core * 4 + col
    place = mine * GROUPS + me

    def owner(k):
        return (mine * 2 + k // 4, lax.rem(k, 4))

    def column(j):
        return (j * 2 + core, col)

    def anywhere(index):
        k = lax.rem(index, GROUPS)
        return ((index // GROUPS) * 2 + k // 4, lax.rem(k, 4))

    def other(j):
        return lax.rem(me + j, GROUPS)

    def other_super(j):
        return lax.rem(mine + j, supers)

    total_places = supers * GROUPS
    after = anywhere(lax.rem(place + 1, total_places))
    before = anywhere(lax.rem(place + total_places - 1, total_places))

    def val_copy(g):
        columns = pl.ds(pl.multiple_of(g * channels, channels), channels)
        return pltpu.make_async_copy(values_hbm.at[:, columns], vals.at[:, columns], val_sem.at[g])

    gate_copy = pltpu.make_async_copy(gate_hbm, gate, gate_sem)

    @pl.loop(0, GROUPS)
    def _(j):
        val_copy(other(j + 1)).start()

    gate_copy.start()

    def remote(src, dst, ss, rs, device):
        return pltpu.make_async_remote_copy(
            src_ref=src, dst_ref=dst, send_sem=ss, recv_sem=rs, device_id=device, device_id_type=MESH
        )

    halo_copy = remote(halo_in, halo_rx, halo_sem.at[0], halo_sem.at[1], after)

    def sig_out(g, c):
        return remote(sig_send.at[g, c], sig_recv.at[me, c], sig_ss.at[g, c], sig_rs.at[me, c], owner(g))

    def sig_in(k, c):
        return remote(sig_send.at[k, c], sig_recv.at[k, c], sig_ss.at[k, c], sig_rs.at[k, c], owner(k))

    def fac_out(g):
        return remote(fac_send.at[g], fac_recv.at[me], fac_ss.at[g], fac_rs.at[me], owner(g))

    def fac_arrive(k):
        return remote(fac_send.at[k], fac_recv.at[k], fac_ss.at[k], fac_rs.at[k], owner(k))

    def stp_out(g):
        return remote(step_in.at[g], stp_recv.at[me], stp_ss.at[g], stp_rs.at[me], owner(g))

    def stp_arrive(k):
        return remote(step_in.at[k], stp_recv.at[k], stp_ss.at[k], stp_rs.at[k], owner(k))

    def d_out(j):
        return remote(
            g_s.at[GROUPS - 1, pl.ds(SPAN - 16, 16)], d_recv.at[mine], d_ss.at[j], d_rs.at[mine], column(j)
        )

    def d_arrive(j):
        return remote(
            g_s.at[GROUPS - 1, pl.ds(SPAN - 16, 16)], d_recv.at[j], d_ss.at[j], d_rs.at[j], column(j)
        )

    def part_of(j):
        return pl.ds(pl.multiple_of(j * slice_rows, slice_rows), slice_rows)

    def st_out(j, c):
        return remote(
            s_send.at[c, part_of(j)], st_recv.at[c, mine], st_ss.at[c, j], st_rs.at[c, mine], column(j)
        )

    def st_arrive(j, c):
        return remote(s_send.at[c, part_of(j)], st_recv.at[c, j], st_ss.at[c, j], st_rs.at[c, j], column(j))

    def e_out(j, c):
        return remote(
            e_send.at[c, j], e_recv.at[c, part_of(mine)], e_ss.at[c, j], e_rs.at[c, mine], column(j)
        )

    def e_arrive(j, c):
        return remote(e_send.at[c, j], e_recv.at[c, part_of(j)], e_ss.at[c, j], e_rs.at[c, j], column(j))

    def y_out(k, c):
        return remote(sig_send.at[k, c], y_recv.at[me, c], y_ss.at[k, c], y_rs.at[me, c], owner(k))

    def y_arrive(k, c):
        return remote(sig_send.at[k, c], y_recv.at[k, c], y_ss.at[k, c], y_rs.at[k, c], owner(k))

    barrier = pltpu.get_barrier_semaphore()

    @pl.loop(1, GROUPS)
    def _(j):
        pl.semaphore_signal(barrier, inc=1, device_id=owner(other(j)), device_id_type=MESH)

    @pl.loop(1, supers)
    def _(j):
        pl.semaphore_signal(barrier, inc=1, device_id=column(other_super(j)), device_id_type=MESH)

    pl.semaphore_signal(barrier, inc=1, device_id=after, device_id_type=MESH)
    pl.semaphore_signal(barrier, inc=1, device_id=before, device_id_type=MESH)
    pl.semaphore_wait(barrier, GROUPS - 1 + supers - 1 + 2)

    halo_copy.start()

    @pl.loop(1, GROUPS)
    def _(j):
        stp_out(other(j)).start()

    stp_recv[me] = step_in[me]

    slot = lax.broadcasted_iota(jnp.int32, (128, channels), 0)
    channel = lax.broadcasted_iota(jnp.int32, (128, channels), 1)
    hit = jnp.zeros((128, channels), F32)
    for piece in range(3):
        hit = jnp.where(slot == channel // HEAD_DIM + piece * heads, 1.0, hit)
    expander[...] = hit.astype(BF16)

    def expand(columns, c, lb):
        return jnp.dot(
            columns, expander[:, c * width + lb : c * width + lb + lanes], preferred_element_type=F32
        )

    halo_copy.wait_recv()
    arrived = jnp.where(place > 0, halo_rx[...].astype(F32), 0.0)
    quarter = GROUPS * channels // 4
    quarter_f = GROUPS * 2 * STATE // 4
    for row in range(1, CONV):
        for q in range(4):
            line = arrived[row * 4 + q : row * 4 + q + 1]
            halo_v[4 + row : 5 + row, q * quarter : (q + 1) * quarter] = line[:, :quarter]
            halo_f[4 + row : 5 + row, q * quarter_f : (q + 1) * quarter_f] = line[:, quarter:]

    def factors_of(g, target):
        for lb in range(0, 2 * STATE, LANES):
            here = pl.ds(pl.multiple_of(g * (2 * STATE) + lb, LANES), LANES)
            target[:, lb : lb + LANES] = convolved(
                fac_in[g, :, lb : lb + LANES].astype(F32), halo_f[:, here], conv_f[:, here]
            )

    @pl.loop(1, GROUPS)
    def _(j):
        g = other(j)
        factors_of(g, fac_send.at[g])
        fac_out(g).start()

    factors_of(me, fac_recv.at[me])

    def signal_of(g, c, target):
        @pl.loop(0, width // lanes)
        def _(i):
            lb = pl.multiple_of(i * lanes, lanes)
            here = pl.ds(pl.multiple_of(g * channels + c * width + lb, lanes), lanes)
            target[:, pl.ds(lb, lanes)] = convolved(
                vals[:, here].astype(F32), halo_v[:, here], conv_v[:, here]
            )

    def signals(c, send):
        @pl.loop(1, GROUPS)
        def _(j):
            g = other(j)
            if c == 0:
                val_copy(g).wait()
            signal_of(g, c, sig_send.at[g, c])
            if send:
                sig_out(g, c).start()

        if c == 0:
            val_copy(me).wait()
        signal_of(me, c, sig_recv.at[me, c])

    for c in range(AHEAD):
        signals(c, True)

    @pl.loop(1, GROUPS)
    def _(j):
        stp_arrive(other(j)).wait_recv()

    steps = softplus_below_zero(stp_recv[...].astype(F32))
    step_t[...] = steps
    falls = (steps * jnp.exp(decay[me])[None]).reshape(GROUPS * heads, SPAN)
    upto = (
        lax.broadcasted_iota(jnp.int32, (SPAN, SPAN), 0)
        <= lax.broadcasted_iota(jnp.int32, (SPAN, SPAN), 1)
    ).astype(F32)
    run_t[...] = -jnp.dot(
        falls, upto, preferred_element_type=F32, precision=lax.Precision.HIGHEST
    ).reshape(GROUPS, heads, SPAN)

    def columns_of(k, prior):
        running = run_t[k]
        ending = running[:, SPAN - 1 : SPAN]
        w_s[k] = split_columns(jnp.exp(ending - running) * step_t[k])
        t_s[k] = split_columns(jnp.exp(running))
        g_s[k] = split_columns(jnp.exp(running + prior))
        run_c[k] = jnp.transpose(
            jnp.concatenate([running, jnp.zeros((128 - heads, SPAN), F32)], axis=0)
        )
        return prior + ending

    lax.fori_loop(0, GROUPS, columns_of, jnp.zeros((heads, 1), F32))

    @pl.loop(1, supers)
    def _(j):
        d_out(other_super(j)).start()

    d_recv[mine] = g_s[GROUPS - 1, SPAN - 16 : SPAN, :]

    @pl.loop(1, GROUPS)
    def _(j):
        fac_arrive(other(j)).wait_recv()

    causal = lax.broadcasted_iota(jnp.int32, (SPAN, SPAN), 0) >= lax.broadcasted_iota(
        jnp.int32, (SPAN, SPAN), 1
    )

    @pl.loop(0, GROUPS)
    def _(k):
        b_rows = fac_recv[k, :, 0:STATE]
        turned = jnp.transpose(b_rows.astype(F32)).astype(BF16)
        b_t[k] = turned
        scores[k] = jnp.where(
            causal, jnp.dot(fac_recv[k, :, STATE:], turned, preferred_element_type=F32), 0.0
        )

    for c in range(AHEAD, CHUNKS):
        signals(c, False)

    def wait_chunk(c):
        @pl.loop(1, GROUPS)
        def _(j):
            sig_out(other(j), c).wait_send()
            if c + AHEAD < CHUNKS:
                sig_out(other(j), c + AHEAD).start()

        @pl.loop(1, GROUPS)
        def _(j):
            sig_in(other(j), c).wait_recv()

    def accumulate(c):
        state[...] = jnp.zeros_like(state)

        @pl.loop(0, GROUPS)
        def _(k):
            for lb in range(0, width, lanes):
                here = slice(lb, lb + lanes)
                weight = expand(w_s[k], c, lb)
                weighted[:, here] = (weight * sig_recv[k, c, :, here].astype(F32)).astype(BF16)
                ending = expand(t_s[k, SPAN - 16 : SPAN, :], c, lb)[15:16]
                held = state[:, here]
                local_entry[k, :, here] = held.astype(BF16)
                state[:, here] = held * ending + jnp.dot(
                    b_t[k], weighted[:, here], preferred_element_type=F32
                )

        s_send[c] = state[...].astype(BF16)

        @pl.loop(1, supers)
        def _(j):
            st_out(other_super(j), c).start()

        st_recv[c, mine] = s_send[c, part_of(mine), :]

    def inside(c):
        low_half = lax.broadcasted_iota(jnp.int32, (SPAN, 128), 1) < HEAD_DIM

        @pl.loop(0, GROUPS)
        def _(k):
            for pair in range(chunk_heads // 2):
                here = slice(pair * 128, pair * 128 + 128)
                there = slice(c * width + pair * 128, c * width + pair * 128 + 128)
                mixes = []
                for h in (c * chunk_heads + 2 * pair, c * chunk_heads + 2 * pair + 1):
                    gap = run_c[k, :, h : h + 1] - run_t[k, h : h + 1, :]
                    mixes.append(
                        (jnp.exp(jnp.minimum(gap, 0.0)) * step_t[k, h : h + 1, :] * scores[k]).astype(BF16)
                    )
                signal = sig_recv[k, c, :, here].astype(F32)
                both = jnp.concatenate(
                    [
                        jnp.where(low_half, signal, 0.0).astype(BF16),
                        jnp.where(low_half, 0.0, signal).astype(BF16),
                    ],
                    axis=0,
                )
                part[k, :, there] = (
                    jnp.dot(jnp.concatenate(mixes, axis=1), both, preferred_element_type=F32)
                    + skip[me, :, there] * signal
                )
            for lb in range(0, width, lanes):
                there = slice(c * width + lb, c * width + lb + lanes)
                held = jnp.dot(
                    fac_recv[k, :, STATE:], local_entry[k, :, lb : lb + lanes], preferred_element_type=F32
                )
                part[k, :, there] = part[k, :, there] + expand(t_s[k], c, lb) * held

    def exchange(c):
        if c == 0:

            @pl.loop(1, supers)
            def _(j):
                d_arrive(other_super(j)).wait_recv()

            for j in range(supers):
                d_wide[j : j + 1, :] = jnp.dot(
                    d_recv[j], expander[...], preferred_element_type=F32
                )[15:16]

        @pl.loop(1, supers)
        def _(j):
            st_arrive(other_super(j), c).wait_recv()

        entry = jnp.zeros((slice_rows, width), F32)
        for j in range(supers):
            e_send[c, j] = entry.astype(BF16)
            if j + 1 < supers:
                entry = entry * d_wide[j : j + 1, c * width : (c + 1) * width] + st_recv[c, j].astype(F32)

        @pl.loop(1, supers)
        def _(j):
            e_out(other_super(j), c).start()

        e_recv[c, part_of(mine), :] = e_send[c, mine]

    def results(c):
        @pl.loop(1, supers)
        def _(j):
            e_arrive(other_super(j), c).wait_recv()

        def result_of(k, target):
            for lb in range(0, width, lanes):
                there = slice(c * width + lb, c * width + lb + lanes)
                held = jnp.dot(
                    fac_recv[k, :, STATE:], e_recv[c, :, lb : lb + lanes], preferred_element_type=F32
                )
                target[:, lb : lb + lanes] = (
                    part[k, :, there] + expand(g_s[k], c, lb) * held
                ).astype(BF16)

        @pl.loop(1, GROUPS)
        def _(j):
            k = other(j)
            result_of(k, sig_send.at[k, c])
            y_out(k, c).start()

        result_of(me, y_recv.at[me, c])

    def out_copy(k):
        columns = pl.ds(pl.multiple_of(k * channels, channels), channels)
        return pltpu.make_async_copy(vals.at[:, columns], out_hbm.at[:, columns], out_sem.at[k])

    def finish(c):
        if c == 0:
            gate_copy.wait()

        @pl.loop(0, GROUPS)
        def _(j):
            k = other(j)

            @pl.when(j > 0)
            def _():
                y_arrive(k, c).wait_recv()

            total = jnp.zeros((SPAN, 128), F32)
            if c > 0:
                total = squares[k]
            for lb in range(0, width, lanes):
                here = pl.ds(pl.multiple_of(k * channels + c * width + lb, lanes), lanes)
                value = y_recv[k, c, :, lb : lb + lanes].astype(F32) * silu_wide(
                    gate[:, here].astype(F32)
                )
                gated[k, :, c * width + lb : c * width + lb + lanes] = value
                square = value * value
                for start in range(0, lanes, 128):
                    total = total + square[:, start : start + 128]
            if c + 1 < CHUNKS:
                squares[k] = total
            else:
                mean = jnp.sum(total, axis=1, keepdims=True) * (1.0 / channels)
                inverse = lax.rsqrt(mean + 1e-05)
                for lb in range(0, channels, LANES):
                    here = pl.ds(pl.multiple_of(k * channels + lb, LANES), LANES)
                    vals[:, here] = (
                        gated[k, :, lb : lb + LANES] * inverse * gain[k, :, lb : lb + LANES]
                    ).astype(BF16)
                out_copy(k).start()

    wait_chunk(0)
    accumulate(0)
    inside(0)
    exchange(0)
    for c in range(1, CHUNKS):
        wait_chunk(c)
        accumulate(c)
        results(c - 1)
        inside(c)
        exchange(c)
        if c >= 2:
            finish(c - 2)
    if CHUNKS >= 2:
        finish(CHUNKS - 2)
    results(CHUNKS - 1)
    finish(CHUNKS - 1)

    halo_copy.wait_send()

    @pl.loop(1, GROUPS)
    def _(j):
        g = other(j)
        stp_out(g).wait_send()
        fac_out(g).wait_send()
        for c in range(CHUNKS):
            y_out(g, c).wait_send()

    @pl.loop(1, supers)
    def _(j):
        peer = other_super(j)
        d_out(peer).wait_send()
        for c in range(CHUNKS):
            st_out(peer, c).wait_send()
            e_out(peer, c).wait_send()

    @pl.loop(0, GROUPS)
    def _(j):
        out_copy(other(j)).wait()


def local(
    values_in, factors_in, step_raw, gate_in, conv_values, conv_factors, decay_log, skip_gain, norm_gain
):
    rows, inner = values_in.shape
    heads = step_raw.shape[1] // GROUPS
    channels = heads * HEAD_DIM
    width = channels // CHUNKS
    supers = lax.axis_size("seq") // 2
    slice_rows = STATE // supers
    wide = GROUPS * 2 * STATE

    fac = jnp.transpose(factors_in.reshape(rows, GROUPS, 2 * STATE), (1, 0, 2))
    step_in = jnp.transpose(step_raw).reshape(GROUPS, heads, rows)
    halo = jnp.concatenate(
        [
            values_in[rows - 4 :].reshape(16, inner // 4),
            factors_in[rows - 4 :].reshape(16, wide // 4),
        ],
        axis=1,
    )
    conv_v = conv_values.astype(F32)
    conv_f = conv_factors.reshape(CONV, wide).astype(F32)
    decay = jnp.broadcast_to(decay_log.reshape(GROUPS, heads, 1), (GROUPS, heads, SPAN))
    skip = jnp.repeat(skip_gain, HEAD_DIM).reshape(GROUPS, 1, channels)
    gain = norm_gain.reshape(GROUPS, 1, channels)

    vmem = pl.BlockSpec(memory_space=pltpu.VMEM)
    hbm = pl.BlockSpec(memory_space=pl.ANY)
    dma = pltpu.SemaphoreType.DMA
    scratch = [
        pltpu.VMEM((SPAN, inner), BF16),
        pltpu.VMEM((SPAN, inner), BF16),
        pltpu.VMEM(halo.shape, BF16),
        pltpu.VMEM((8, inner), F32),
        pltpu.VMEM((8, wide), F32),
        pltpu.VMEM((GROUPS, CHUNKS, SPAN, width), BF16),
        pltpu.VMEM((GROUPS, CHUNKS, SPAN, width), BF16),
        pltpu.VMEM((GROUPS, SPAN, 2 * STATE), BF16),
        pltpu.VMEM((GROUPS, SPAN, 2 * STATE), BF16),
        pltpu.VMEM((GROUPS, heads, SPAN), BF16),
        pltpu.VMEM((GROUPS, heads, SPAN), F32),
        pltpu.VMEM((GROUPS, heads, SPAN), F32),
        pltpu.VMEM((GROUPS, SPAN, 128), F32),
        pltpu.VMEM((GROUPS, SPAN, 128), BF16),
        pltpu.VMEM((GROUPS, SPAN, 128), BF16),
        pltpu.VMEM((GROUPS, SPAN, 128), BF16),
        pltpu.VMEM((GROUPS, STATE, SPAN), BF16),
        pltpu.VMEM((GROUPS, SPAN, SPAN), F32),
        pltpu.VMEM((128, channels), BF16),
        pltpu.VMEM((STATE, width), F32),
        pltpu.VMEM((GROUPS, STATE, width), BF16),
        pltpu.VMEM((CHUNKS, STATE, width), BF16),
        pltpu.VMEM((CHUNKS, supers, slice_rows, width), BF16),
        pltpu.VMEM((CHUNKS, supers, slice_rows, width), BF16),
        pltpu.VMEM((CHUNKS, STATE, width), BF16),
        pltpu.VMEM((supers, 16, 128), BF16),
        pltpu.VMEM((max(supers, 8), channels), F32),
        pltpu.VMEM((GROUPS, SPAN, channels), F32),
        pltpu.VMEM((SPAN, width), BF16),
        pltpu.VMEM((GROUPS, SPAN, channels), F32),
        pltpu.VMEM((GROUPS, SPAN, 128), F32),
        pltpu.VMEM((GROUPS, CHUNKS, SPAN, width), BF16),
        dma((GROUPS,)), dma, dma((GROUPS,)), dma((2,)),
        dma((GROUPS, CHUNKS)), dma((GROUPS, CHUNKS)),
        dma((GROUPS,)), dma((GROUPS,)),
        dma((GROUPS,)), dma((GROUPS,)),
        dma((supers,)), dma((supers,)),
        dma((CHUNKS, supers)), dma((CHUNKS, supers)),
        dma((CHUNKS, supers)), dma((CHUNKS, supers)),
        dma((GROUPS, CHUNKS)), dma((GROUPS, CHUNKS)),
    ]
    return pl.pallas_call(
        partial(body, heads=heads, supers=supers),
        out_shape=jax.ShapeDtypeStruct((rows, inner), BF16),
        in_specs=[hbm, hbm] + [vmem] * 8,
        out_specs=hbm,
        scratch_shapes=scratch,
        compiler_params=pltpu.CompilerParams(
            collective_id=0, has_side_effects=True, vmem_limit_bytes=61 * 2**20
        ),
        name="layer",
    )(values_in, gate_in, fac, step_in, halo, conv_v, conv_f, decay, skip, gain)


def solution(mesh):
    rows = P(("seq", "head"), None)
    placed = (rows, P(("seq", "head"), None, None, None), rows, rows, P(), P(), P(), P(), P())
    return jax.shard_map(local, mesh=mesh, in_specs=placed, out_specs=rows, check_vma=False)
```

time: 879 us -> 147 us (0.17)
  waiting for transfers between devices: 441 us -> 0 us
  other arithmetic: 236 us -> 2.29 us
  Pallas kernels: 0 us -> 129 us
  local copies, waits for them, and re-layouts: 85 us -> 15.6 us
  matrix products: 50.3 us -> 0 us
  blocking collectives: 25.4 us -> 0 us
  starting transfers between devices: 25 us -> 0 us
  between operations: 13.7 us -> 0.05 us
    all_gather x1 -> x0, waiting for transfers between devices: 349 us -> none  [prefix(): pieces = jax.tree.map(lambda part: lax.all_gather(part, axis), value)]
    select_n x32 -> x0, other arithmetic: 185 us -> none  [the longest x31 185 us: hop(): jnp.where(position < mine, new, old)]
    pallas_call x0 -> x1, Pallas kernels: none -> 129 us  [local(): pl.pallas_call(partial(body, heads=heads, supers=supers), out_shape=jax.S...]
    all_to_all x4 -> x0, waiting for transfers between devices: 91.9 us -> none  [the longest x1 48.7 us: local(): lax.all_to_all(signal_rows, 'head', split_axis=1, concat_axis=0, tiled=True)]
    dot_general x13 -> x0, matrix products: 50.3 us -> none  [the longest x4 19.7 us: block_terms(): jnp.einsum('sgjp,sgn->gjpn', weighted, b_factor, preferred_element_type=j...]
    unnamed x15 -> x1, local copies, waits for them, and re-layouts: 35.3 us -> 4.57 us
    convert_element_type x5 -> x1, other arithmetic: 29 us -> 1.62 us  [local(): conv_v = conv_values.astype(F32)]
    all_gather x1 -> x0, blocking collectives: 25.4 us -> none  [prefix(): pieces = jax.tree.map(lambda part: lax.all_gather(part, axis), value)]
  transfers between devices with their start and end apart: 7 -> 0, of which waited for: 3 -> 0; matrix products, arithmetic and copies ran while one was open for 5% -> 0% of each run, Pallas kernels for 0% -> 0%
where the time goes in v1:
time: 147 us; the launch traced here: 146 us
  Pallas kernels  129 us (88%)
  local copies, waits for them, and re-layouts  15.6 us (11%)
  other arithmetic  2.29 us (2%)
    pallas_call x1, Pallas kernels, local(): pl.pallas_call(partial(body, heads=heads, supers=supers), out_shape=jax.S...  129 us
    unnamed x1, local copies, waits for them, and re-layouts  4.57 us
    reshape x2, local copies, waits for them, and re-layouts, local(): fac = jnp.transpose(factors_in.reshape(rows, GROUPS, 2 * STATE), (1, 0, 2))  3.02 us

profile of v1, /device:TPU:0, one launch (start us, length us, event | category | flops | bytes accessed | tf_op | source)
XLA Modules:
  0.0 146.4 jit_solution(16085195912190529805)
XLA Ops:
  0.0 0.8 broadcast_in_dim.14
  0.8 0.8 broadcast_in_dim.16
  1.5 0.8 slice.7
  2.3 1.6 %copy.11 = bf16[256,128]{1,0:T(8,128)(2,1)} copy(bf16[256,128]{0,1:T(8,128)(2,1)} %bitcast.9) | data formatting | bytes 131072 | tf_op jit(solution)/shard_map/transpose | solution.py:528
  3.9 1.4 reshape.32.conv_f
  5.3 0.1 broadcast_in_dim.17
  5.4 0.7 broadcast_in_dim.18.skip
  6.1 0.8 broadcast_in_dim.15.decay
  6.9 1.0 slice.6
  7.9 0.1 reshape.29
  8.0 0.7 pad_maximum_fusion.halo_in
  8.7 1.6 %convert_element_type.8.conv_v = f32[4,16384]{1,0:T(4,128)} convert(bf16[4,16384]{1,0:T(4,128)(2,1)} %param.13) | non-fusion elementwise | flops 65536 | bytes 393216 | tf_op jit(solution)/shard_map/convert_element_type | solution.py:536
  10.3 1.7 %reshape.33 = bf16[128,8,512]{2,1,0:T(8,128)(2,1)S(1)} reshape(bf16[128,8,2,256]{3,2,1,0:T(2,128)(2,1)} %param.10) | data formatting | bytes 2097152 | tf_op jit(solution)/shard_map/reshape | solution.py:527
  12.0 1.3 copy.14
  13.3 128.5 %layer.1 = bf16[128,16384]{1,0:T(8,128)(2,1)} custom-call(bf16[128,16384]{1,0:T(8,128)(2,1)} %values_hbm.1, bf16[128,16384]{1,0:T(8,128)(2,1)} %gate_hbm.1, bf16[8,128,512]{2,1,0:T(8,128)(2,1)} %bitcast.6, bf16[8,32,128]{2,1,0:T(8,128)(2,1)} %bitcast.7, bf16[16,5120]{1,0:T(8,128)(2,1)} %pad_maximum_fusion.halo_in, f32[4,16384]{1,0:T(4,128)} %convert_element_type.8.conv_v, ...), custom_call_target="tpu_custom_call" | custom-call | tf_op jit(solution)/shard_map/layer/pallas_call | solution.py:587
  141.9 4.6 %copy.16 = bf16[128,16384]{1,0:T(8,128)(2,1)} copy(bf16[128,16384]{1,0:T(8,128)(2,1)} %layer.1) | data formatting | bytes 8388608
  (1 shorter events, 0.0 us)

commit v2 on v1

--- a/solution.py
+++ b/solution.py
@@ -13,7 +13,7 @@
 SPAN = 128
 CONV = 4
 CHUNKS = 4
-AHEAD = 2
+AHEAD = 4
 LANES = 256
 F32 = jnp.float32
 BF16 = jnp.bfloat16
@@ -59,14 +59,13 @@
 
 
 def body(
-    values_hbm, gate_hbm, fac_in, step_in, halo_in, conv_v, conv_f, decay, skip, gain,
+    values_hbm, gate_hbm, fac_hbm, step_in, conv_v, conv_f, decay, skip, gain,
     out_hbm,
-    vals, gate, halo_rx, halo_v, halo_f,
-    sig_send, sig_recv, fac_send, fac_recv, stp_recv,
-    step_t, run_t, run_c, w_s, t_s, g_s, b_t, scores, expander,
+    out, gate, tail_v, tail_f, raw_v, raw_f, signal, b_rows, c_rows, stp_send, stp_recv,
+    head_col, skip_row, step_t, run_t, run_c, w_s, t_s, g_s, b_t, scores, expander,
     state, local_entry, s_send, st_recv, e_send, e_recv, d_recv, d_wide,
-    part, weighted, gated, squares, y_recv,
-    val_sem, gate_sem, out_sem, halo_sem,
+    part, weighted, gated, squares, y_send, y_recv,
+    own_sem, gate_sem, out_sem, tail_ss, tail_rs,
     sig_ss, sig_rs, fac_ss, fac_rs, stp_ss, stp_rs, d_ss, d_rs,
     st_ss, st_rs, e_ss, e_rs, y_ss, y_rs,
     *, heads, supers,
@@ -99,46 +98,57 @@
     def other_super(j):
         return lax.rem(mine + j, supers)
 
-    total_places = supers * GROUPS
-    after = anywhere(lax.rem(place + 1, total_places))
-    before = anywhere(lax.rem(place + total_places - 1, total_places))
-
-    def val_copy(g):
-        columns = pl.ds(pl.multiple_of(g * channels, channels), channels)
-        return pltpu.make_async_copy(values_hbm.at[:, columns], vals.at[:, columns], val_sem.at[g])
-
+    following = column(other_super(1))
+    previous = column(other_super(supers - 1))
+
+    def columns_of_chunk(g, c):
+        return pl.ds(pl.multiple_of(g * channels + c * width, width), width)
+
+    def own_copy(c):
+        return pltpu.make_async_copy(
+            values_hbm.at[:, columns_of_chunk(me, c)], raw_v.at[me, c], own_sem.at[c]
+        )
+
+    own_factors = pltpu.make_async_copy(fac_hbm.at[me], raw_f.at[me], own_sem.at[CHUNKS])
     gate_copy = pltpu.make_async_copy(gate_hbm, gate, gate_sem)
-
-    @pl.loop(0, GROUPS)
-    def _(j):
-        val_copy(other(j + 1)).start()
-
-    gate_copy.start()
 
     def remote(src, dst, ss, rs, device):
         return pltpu.make_async_remote_copy(
             src_ref=src, dst_ref=dst, send_sem=ss, recv_sem=rs, device_id=device, device_id_type=MESH
         )
 
-    halo_copy = remote(halo_in, halo_rx, halo_sem.at[0], halo_sem.at[1], after)
-
     def sig_out(g, c):
-        return remote(sig_send.at[g, c], sig_recv.at[me, c], sig_ss.at[g, c], sig_rs.at[me, c], owner(g))
+        return remote(
+            values_hbm.at[:, columns_of_chunk(g, c)], raw_v.at[me, c], sig_ss.at[g, c], sig_rs.at[me, c], owner(g)
+        )
 
     def sig_in(k, c):
-        return remote(sig_send.at[k, c], sig_recv.at[k, c], sig_ss.at[k, c], sig_rs.at[k, c], owner(k))
+        return remote(
+            values_hbm.at[:, columns_of_chunk(k, c)], raw_v.at[k, c], sig_ss.at[k, c], sig_rs.at[k, c], owner(k)
+        )
 
     def fac_out(g):
-        return remote(fac_send.at[g], fac_recv.at[me], fac_ss.at[g], fac_rs.at[me], owner(g))
+        return remote(fac_hbm.at[g], raw_f.at[me], fac_ss.at[g], fac_rs.at[me], owner(g))
 
     def fac_arrive(k):
-        return remote(fac_send.at[k], fac_recv.at[k], fac_ss.at[k], fac_rs.at[k], owner(k))
+        return remote(fac_hbm.at[k], raw_f.at[k], fac_ss.at[k], fac_rs.at[k], owner(k))
+
+    last_rows = pl.ds(SPAN - 16, 16)
+
+    def tail_v_copy(c):
+        return remote(
+            raw_v.at[GROUPS - 1, c, last_rows], tail_v.at[c], tail_ss.at[c], tail_rs.at[c], following
+        )
+
+    tail_f_copy = remote(
+        raw_f.at[GROUPS - 1, :, last_rows], tail_f, tail_ss.at[CHUNKS], tail_rs.at[CHUNKS], following
+    )
 
     def stp_out(g):
-        return remote(step_in.at[g], stp_recv.at[me], stp_ss.at[g], stp_rs.at[me], owner(g))
+        return remote(stp_send.at[g], stp_recv.at[me], stp_ss.at[g], stp_rs.at[me], owner(g))
 
     def stp_arrive(k):
-        return remote(step_in.at[k], stp_recv.at[k], stp_ss.at[k], stp_rs.at[k], owner(k))
+        return remote(stp_send.at[k], stp_recv.at[k], stp_ss.at[k], stp_rs.at[k], owner(k))
 
     def d_out(j):
         return remote(
@@ -170,10 +180,10 @@
         return remote(e_send.at[c, j], e_recv.at[c, part_of(j)], e_ss.at[c, j], e_rs.at[c, j], column(j))
 
     def y_out(k, c):
-        return remote(sig_send.at[k, c], y_recv.at[me, c], y_ss.at[k, c], y_rs.at[me, c], owner(k))
+        return remote(y_send.at[k, c], y_recv.at[me, c], y_ss.at[k, c], y_rs.at[me, c], owner(k))
 
     def y_arrive(k, c):
-        return remote(sig_send.at[k, c], y_recv.at[k, c], y_ss.at[k, c], y_rs.at[k, c], owner(k))
+        return remote(y_send.at[k, c], y_recv.at[k, c], y_ss.at[k, c], y_rs.at[k, c], owner(k))
 
     barrier = pltpu.get_barrier_semaphore()
 
@@ -185,17 +195,41 @@
     def _(j):
         pl.semaphore_signal(barrier, inc=1, device_id=column(other_super(j)), device_id_type=MESH)
 
-    pl.semaphore_signal(barrier, inc=1, device_id=after, device_id_type=MESH)
-    pl.semaphore_signal(barrier, inc=1, device_id=before, device_id_type=MESH)
-    pl.semaphore_wait(barrier, GROUPS - 1 + supers - 1 + 2)
-
-    halo_copy.start()
+    for start in range(0, GROUPS * heads, 128):
+        count = min(128, GROUPS * heads - start)
+        turned = jnp.transpose(step_in[:, start : start + count].astype(F32)).astype(BF16)
+        stp_send[start // heads : (start + count) // heads] = turned.reshape(count // heads, heads, SPAN)
+
+    pl.semaphore_wait(barrier, GROUPS - 1 + supers - 1)
 
     @pl.loop(1, GROUPS)
     def _(j):
         stp_out(other(j)).start()
 
-    stp_recv[me] = step_in[me]
+    @pl.loop(1, GROUPS)
+    def _(j):
+        fac_out(other(j)).start()
+
+    for c in range(AHEAD):
+
+        @pl.loop(1, GROUPS)
+        def _(j):
+            sig_out(other(j), c).start()
+
+    own_factors.start()
+    for c in range(CHUNKS):
+        own_copy(c).start()
+    gate_copy.start()
+
+    stp_recv[me] = stp_send[me]
+
+    def turn_row(row):
+        for start in range(0, GROUPS * heads, 128):
+            count = min(128, GROUPS * heads - start)
+            head_col[start : start + count, :] = jnp.transpose(
+                jnp.broadcast_to(row[:, start : start + count], (128, count))
+            )
+        return head_col[pl.ds(pl.multiple_of(me * heads, heads), heads), :]
 
     slot = lax.broadcasted_iota(jnp.int32, (128, channels), 0)
     channel = lax.broadcasted_iota(jnp.int32, (128, channels), 1)
@@ -209,56 +243,26 @@
             columns, expander[:, c * width + lb : c * width + lb + lanes], preferred_element_type=F32
         )
 
-    halo_copy.wait_recv()
-    arrived = jnp.where(place > 0, halo_rx[...].astype(F32), 0.0)
-    quarter = GROUPS * channels // 4
-    quarter_f = GROUPS * 2 * STATE // 4
-    for row in range(1, CONV):
-        for q in range(4):
-            line = arrived[row * 4 + q : row * 4 + q + 1]
-            halo_v[4 + row : 5 + row, q * quarter : (q + 1) * quarter] = line[:, :quarter]
-            halo_f[4 + row : 5 + row, q * quarter_f : (q + 1) * quarter_f] = line[:, quarter:]
-
-    def factors_of(g, target):
-        for lb in range(0, 2 * STATE, LANES):
-            here = pl.ds(pl.multiple_of(g * (2 * STATE) + lb, LANES), LANES)
-            target[:, lb : lb + LANES] = convolved(
-                fac_in[g, :, lb : lb + LANES].astype(F32), halo_f[:, here], conv_f[:, here]
+    skip_columns = split_columns(turn_row(skip))
+    for lb in range(0, channels, lanes):
+        skip_row[:, lb : lb + lanes] = expand(skip_columns[0:16, :], 0, lb)[0:8]
+    rate = jnp.exp(turn_row(decay))
+
+    def tail_before(rows):
+        return jnp.where(mine > 0, rows.astype(F32), 0.0)
+
+    def signal_of(k, c, before):
+        for lb in range(0, width, lanes):
+            here = slice(lb, lb + lanes)
+            taps = conv_v[:, pl.ds(pl.multiple_of(me * channels + c * width + lb, lanes), lanes)]
+            signal[k, c, :, here] = convolved(
+                raw_v[k, c, :, here].astype(F32), before(here), taps.astype(F32)
             )
 
-    @pl.loop(1, GROUPS)
-    def _(j):
-        g = other(j)
-        factors_of(g, fac_send.at[g])
-        fac_out(g).start()
-
-    factors_of(me, fac_recv.at[me])
-
-    def signal_of(g, c, target):
-        @pl.loop(0, width // lanes)
-        def _(i):
-            lb = pl.multiple_of(i * lanes, lanes)
-            here = pl.ds(pl.multiple_of(g * channels + c * width + lb, lanes), lanes)
-            target[:, pl.ds(lb, lanes)] = convolved(
-                vals[:, here].astype(F32), halo_v[:, here], conv_v[:, here]
-            )
-
-    def signals(c, send):
-        @pl.loop(1, GROUPS)
-        def _(j):
-            g = other(j)
-            if c == 0:
-                val_copy(g).wait()
-            signal_of(g, c, sig_send.at[g, c])
-            if send:
-                sig_out(g, c).start()
-
-        if c == 0:
-            val_copy(me).wait()
-        signal_of(me, c, sig_recv.at[me, c])
-
-    for c in range(AHEAD):
-        signals(c, True)
+    def factors_of(k, before):
+        for part_index, target in ((0, b_rows), (1, c_rows)):
+            taps = conv_f[:, me, part_index, :].astype(F32)
+            target[k] = convolved(raw_f[k, part_index].astype(F32), before(part_index), taps)
 
     @pl.loop(1, GROUPS)
     def _(j):
@@ -266,7 +270,7 @@
 
     steps = softplus_below_zero(stp_recv[...].astype(F32))
     step_t[...] = steps
-    falls = (steps * jnp.exp(decay[me])[None]).reshape(GROUPS * heads, SPAN)
+    falls = (steps * rate[None]).reshape(GROUPS * heads, SPAN)
     upto = (
         lax.broadcasted_iota(jnp.int32, (SPAN, SPAN), 0)
         <= lax.broadcasted_iota(jnp.int32, (SPAN, SPAN), 1)
@@ -298,21 +302,26 @@
     def _(j):
         fac_arrive(other(j)).wait_recv()
 
+    own_factors.wait()
+    tail_f_copy.start()
+
     causal = lax.broadcasted_iota(jnp.int32, (SPAN, SPAN), 0) >= lax.broadcasted_iota(
         jnp.int32, (SPAN, SPAN), 1
     )
 
-    @pl.loop(0, GROUPS)
+    def scores_of(k):
+        turned = jnp.transpose(b_rows[k].astype(F32)).astype(BF16)
+        b_t[k] = turned
+        scores[k] = jnp.where(causal, jnp.dot(c_rows[k], turned, preferred_element_type=F32), 0.0)
+
+    @pl.loop(1, GROUPS)
     def _(k):
-        b_rows = fac_recv[k, :, 0:STATE]
-        turned = jnp.transpose(b_rows.astype(F32)).astype(BF16)
-        b_t[k] = turned
-        scores[k] = jnp.where(
-            causal, jnp.dot(fac_recv[k, :, STATE:], turned, preferred_element_type=F32), 0.0
-        )
-
-    for c in range(AHEAD, CHUNKS):
-        signals(c, False)
+        factors_of(k, lambda i: raw_f[k - 1, i, SPAN - 16 : SPAN, :].astype(F32)[8:16])
+        scores_of(k)
+
+    tail_f_copy.wait_recv()
+    factors_of(0, lambda i: tail_before(tail_f[i])[8:16])
+    scores_of(0)
 
     def wait_chunk(c):
         @pl.loop(1, GROUPS)
@@ -324,6 +333,16 @@
         @pl.loop(1, GROUPS)
         def _(j):
             sig_in(other(j), c).wait_recv()
+
+        own_copy(c).wait()
+        tail_v_copy(c).start()
+
+        @pl.loop(1, GROUPS)
+        def _(k):
+            signal_of(k, c, lambda here: raw_v[k - 1, c, SPAN - 16 : SPAN, here].astype(F32)[8:16])
+
+        tail_v_copy(c).wait_recv()
+        signal_of(0, c, lambda here: tail_before(tail_v[c, :, here])[8:16])
 
     def accumulate(c):
         state[...] = jnp.zeros_like(state)
@@ -333,7 +352,7 @@
             for lb in range(0, width, lanes):
                 here = slice(lb, lb + lanes)
                 weight = expand(w_s[k], c, lb)
-                weighted[:, here] = (weight * sig_recv[k, c, :, here].astype(F32)).astype(BF16)
+                weighted[:, here] = (weight * signal[k, c, :, here].astype(F32)).astype(BF16)
                 ending = expand(t_s[k, SPAN - 16 : SPAN, :], c, lb)[15:16]
                 held = state[:, here]
                 local_entry[k, :, here] = held.astype(BF16)
@@ -363,22 +382,22 @@
                     mixes.append(
                         (jnp.exp(jnp.minimum(gap, 0.0)) * step_t[k, h : h + 1, :] * scores[k]).astype(BF16)
                     )
-                signal = sig_recv[k, c, :, here].astype(F32)
+                values = signal[k, c, :, here].astype(F32)
                 both = jnp.concatenate(
                     [
-                        jnp.where(low_half, signal, 0.0).astype(BF16),
-                        jnp.where(low_half, 0.0, signal).astype(BF16),
+                        jnp.where(low_half, values, 0.0).astype(BF16),
+                        jnp.where(low_half, 0.0, values).astype(BF16),
                     ],
                     axis=0,
                 )
                 part[k, :, there] = (
                     jnp.dot(jnp.concatenate(mixes, axis=1), both, preferred_element_type=F32)
-                    + skip[me, :, there] * signal
+                    + skip_row[0:1, there] * values
                 )
             for lb in range(0, width, lanes):
                 there = slice(c * width + lb, c * width + lb + lanes)
                 held = jnp.dot(
-                    fac_recv[k, :, STATE:], local_entry[k, :, lb : lb + lanes], preferred_element_type=F32
+                    c_rows[k], local_entry[k, :, lb : lb + lanes], preferred_element_type=F32
                 )
                 part[k, :, there] = part[k, :, there] + expand(t_s[k], c, lb) * held
 
@@ -419,7 +438,7 @@
             for lb in range(0, width, lanes):
                 there = slice(c * width + lb, c * width + lb + lanes)
                 held = jnp.dot(
-                    fac_recv[k, :, STATE:], e_recv[c, :, lb : lb + lanes], preferred_element_type=F32
+                    c_rows[k], e_recv[c, :, lb : lb + lanes], preferred_element_type=F32
                 )
                 target[:, lb : lb + lanes] = (
                     part[k, :, there] + expand(g_s[k], c, lb) * held
@@ -428,14 +447,14 @@
         @pl.loop(1, GROUPS)
         def _(j):
             k = other(j)
-            result_of(k, sig_send.at[k, c])
+            result_of(k, y_send.at[k, c])
             y_out(k, c).start()
 
         result_of(me, y_recv.at[me, c])
 
     def out_copy(k):
         columns = pl.ds(pl.multiple_of(k * channels, channels), channels)
-        return pltpu.make_async_copy(vals.at[:, columns], out_hbm.at[:, columns], out_sem.at[k])
+        return pltpu.make_async_copy(out.at[:, columns], out_hbm.at[:, columns], out_sem.at[k])
 
     def finish(c):
         if c == 0:
@@ -468,7 +487,7 @@
                 inverse = lax.rsqrt(mean + 1e-05)
                 for lb in range(0, channels, LANES):
                     here = pl.ds(pl.multiple_of(k * channels + lb, LANES), LANES)
-                    vals[:, here] = (
+                    out[:, here] = (
                         gated[k, :, lb : lb + LANES] * inverse * gain[k, :, lb : lb + LANES]
                     ).astype(BF16)
                 out_copy(k).start()
@@ -483,14 +502,13 @@
         results(c - 1)
         inside(c)
         exchange(c)
-        if c >= 2:
-            finish(c - 2)
-    if CHUNKS >= 2:
-        finish(CHUNKS - 2)
     results(CHUNKS - 1)
-    finish(CHUNKS - 1)
-
-    halo_copy.wait_send()
+    for c in range(CHUNKS):
+        finish(c)
+
+    tail_f_copy.wait_send()
+    for c in range(CHUNKS):
+        tail_v_copy(c).wait_send()
 
     @pl.loop(1, GROUPS)
     def _(j):
@@ -522,21 +540,8 @@
     width = channels // CHUNKS
     supers = lax.axis_size("seq") // 2
     slice_rows = STATE // supers
-    wide = GROUPS * 2 * STATE
-
-    fac = jnp.transpose(factors_in.reshape(rows, GROUPS, 2 * STATE), (1, 0, 2))
-    step_in = jnp.transpose(step_raw).reshape(GROUPS, heads, rows)
-    halo = jnp.concatenate(
-        [
-            values_in[rows - 4 :].reshape(16, inner // 4),
-            factors_in[rows - 4 :].reshape(16, wide // 4),
-        ],
-        axis=1,
-    )
-    conv_v = conv_values.astype(F32)
-    conv_f = conv_factors.reshape(CONV, wide).astype(F32)
-    decay = jnp.broadcast_to(decay_log.reshape(GROUPS, heads, 1), (GROUPS, heads, SPAN))
-    skip = jnp.repeat(skip_gain, HEAD_DIM).reshape(GROUPS, 1, channels)
+
+    fac = jnp.transpose(factors_in, (1, 2, 0, 3))
     gain = norm_gain.reshape(GROUPS, 1, channels)
 
     vmem = pl.BlockSpec(memory_space=pltpu.VMEM)
@@ -545,14 +550,17 @@
     scratch = [
         pltpu.VMEM((SPAN, inner), BF16),
         pltpu.VMEM((SPAN, inner), BF16),
-        pltpu.VMEM(halo.shape, BF16),
-        pltpu.VMEM((8, inner), F32),
-        pltpu.VMEM((8, wide), F32),
+        pltpu.VMEM((CHUNKS, 16, width), BF16),
+        pltpu.VMEM((2, 16, STATE), BF16),
         pltpu.VMEM((GROUPS, CHUNKS, SPAN, width), BF16),
+        pltpu.VMEM((GROUPS, 2, SPAN, STATE), BF16),
         pltpu.VMEM((GROUPS, CHUNKS, SPAN, width), BF16),
-        pltpu.VMEM((GROUPS, SPAN, 2 * STATE), BF16),
-        pltpu.VMEM((GROUPS, SPAN, 2 * STATE), BF16),
+        pltpu.VMEM((GROUPS, SPAN, STATE), BF16),
+        pltpu.VMEM((GROUPS, SPAN, STATE), BF16),
         pltpu.VMEM((GROUPS, heads, SPAN), BF16),
+        pltpu.VMEM((GROUPS, heads, SPAN), BF16),
+        pltpu.VMEM((GROUPS * heads, 128), F32),
+        pltpu.VMEM((8, channels), F32),
         pltpu.VMEM((GROUPS, heads, SPAN), F32),
         pltpu.VMEM((GROUPS, heads, SPAN), F32),
         pltpu.VMEM((GROUPS, SPAN, 128), F32),
@@ -575,7 +583,8 @@
         pltpu.VMEM((GROUPS, SPAN, channels), F32),
         pltpu.VMEM((GROUPS, SPAN, 128), F32),
         pltpu.VMEM((GROUPS, CHUNKS, SPAN, width), BF16),
-        dma((GROUPS,)), dma, dma((GROUPS,)), dma((2,)),
+        pltpu.VMEM((GROUPS, CHUNKS, SPAN, width), BF16),
+        dma((CHUNKS + 1,)), dma, dma((GROUPS,)), dma((CHUNKS + 1,)), dma((CHUNKS + 1,)),
         dma((GROUPS, CHUNKS)), dma((GROUPS, CHUNKS)),
         dma((GROUPS,)), dma((GROUPS,)),
         dma((GROUPS,)), dma((GROUPS,)),
@@ -587,14 +596,17 @@
     return pl.pallas_call(
         partial(body, heads=heads, supers=supers),
         out_shape=jax.ShapeDtypeStruct((rows, inner), BF16),
-        in_specs=[hbm, hbm] + [vmem] * 8,
+        in_specs=[hbm, hbm, hbm] + [vmem] * 6,
         out_specs=hbm,
         scratch_shapes=scratch,
         compiler_params=pltpu.CompilerParams(
             collective_id=0, has_side_effects=True, vmem_limit_bytes=61 * 2**20
         ),
         name="layer",
-    )(values_in, gate_in, fac, step_in, halo, conv_v, conv_f, decay, skip, gain)
+    )(
+        values_in, gate_in, fac, step_raw, conv_values, conv_factors,
+        decay_log.reshape(1, -1), skip_gain.reshape(1, -1), gain,
+    )
 
 
 def solution(mesh):

time: 147 us -> 127 us (0.86)
  Pallas kernels: 129 us -> 120 us
  local copies, waits for them, and re-layouts: 15.6 us -> 7.1 us
  other arithmetic: 2.29 us -> 0 us
    pallas_call x1, Pallas kernels: 129 us -> 120 us  [local(): pl.pallas_call(partial(body, heads=heads, supers=supers), out_shape=jax.S...]
    reshape x4 -> x0, local copies, waits for them, and re-layouts: 3.12 us -> none  [the longest x2 3.02 us: local(): fac = jnp.transpose(factors_in.reshape(rows, GROUPS, 2 * STATE), (1, 0, 2))]
    broadcast_in_dim x5 -> x0, local copies, waits for them, and re-layouts: 3.1 us -> none  [the longest x3 1.59 us: local(): skip = jnp.repeat(skip_gain, HEAD_DIM).reshape(GROUPS, 1, channels)]
    unnamed x1 -> x2, local copies, waits for them, and re-layouts: 4.57 us -> 7.1 us
    slice x2 -> x0, local copies, waits for them, and re-layouts: 1.8 us -> none  [the longest x1 1.02 us: local(): values_in[rows - 4:].reshape(16, inner // 4)]
    convert_element_type x1 -> x0, other arithmetic: 1.62 us -> none  [local(): conv_v = conv_values.astype(F32)]
    transpose x1 -> x0, local copies, waits for them, and re-layouts: 1.57 us -> none  [local(): step_in = jnp.transpose(step_raw).reshape(GROUPS, heads, rows)]
where the time goes in v2:
time: 127 us
  Pallas kernels  120 us (94%)
  local copies, waits for them, and re-layouts  7.1 us (6%)
    pallas_call x1, Pallas kernels, local(): pl.pallas_call(partial(body, heads=heads, supers=supers), out_shape=jax.S...  120 us
    unnamed x2, local copies, waits for them, and re-layouts  7.1 us

profile of v2, /device:TPU:0, one launch (start us, length us, event | category | flops | bytes accessed | tf_op | source)
XLA Modules:
  0.0 126.9 jit_solution(2478568865413111319)
XLA Ops:
  0.0 2.5 %copy.12 = bf16[128,8,2,256]{3,0,2,1:T(8,128)(2,1)} copy(bf16[128,8,2,256]{3,2,1,0:T(2,128)(2,1)} %param.10) | data formatting | bytes 2097152 | tf_op args[1]
  2.5 119.8 %layer.1 = bf16[128,16384]{1,0:T(8,128)(2,1)} custom-call(bf16[128,16384]{1,0:T(8,128)(2,1)} %values_hbm.1, bf16[128,16384]{1,0:T(8,128)(2,1)} %gate_hbm.1, bf16[8,2,128,256]{3,2,1,0:T(8,128)(2,1)} %bitcast.6, bf16[128,256]{1,0:T(8,128)(2,1)} %step_in.1, bf16[4,16384]{1,0:T(4,128)(2,1)} %conv_v.1, bf16[4,8,2,256]{3,2,1,0:T(2,128)(2,1)} %conv_f.1, ...), custom_call_target="tpu_custom_call" | custom-call | tf_op jit(solution)/shard_map/layer/pallas_call | solution.py:596
  122.3 4.6 %copy.14 = bf16[128,16384]{1,0:T(8,128)(2,1)} copy(bf16[128,16384]{1,0:T(8,128)(2,1)} %layer.1) | data formatting | bytes 8388608

commit v3 on v2

--- a/solution.py
+++ b/solution.py
@@ -59,15 +59,15 @@
 
 
 def body(
-    values_hbm, gate_hbm, fac_hbm, step_in, conv_v, conv_f, decay, skip, gain,
+    values_hbm, gate_hbm, fac_hbm, step_hbm, conv_v_hbm, conv_f_hbm, decay_hbm, skip_hbm, gain_hbm,
     out_hbm,
-    out, gate, tail_v, tail_f, raw_v, raw_f, signal, b_rows, c_rows, stp_send, stp_recv,
+    step_in, conv_v, conv_f, decay, skip, gain, out, gate, tail_v, tail_f, raw_v, raw_f, signal, b_rows, c_rows, stp_send, stp_recv,
     head_col, skip_row, step_t, run_t, run_c, w_s, t_s, g_s, b_t, scores, expander,
     state, local_entry, s_send, st_recv, e_send, e_recv, d_recv, d_wide,
     part, weighted, gated, squares, y_send, y_recv,
     own_sem, gate_sem, out_sem, tail_ss, tail_rs,
     sig_ss, sig_rs, fac_ss, fac_rs, stp_ss, stp_rs, d_ss, d_rs,
-    st_ss, st_rs, e_ss, e_rs, y_ss, y_rs,
+    st_ss, st_rs, e_ss, e_rs, y_ss, y_rs, met, small_sem,
     *, heads, supers,
 ):
     channels = heads * HEAD_DIM
@@ -109,7 +109,7 @@
             values_hbm.at[:, columns_of_chunk(me, c)], raw_v.at[me, c], own_sem.at[c]
         )
 
-    own_factors = pltpu.make_async_copy(fac_hbm.at[me], raw_f.at[me], own_sem.at[CHUNKS])
+    own_factors = pltpu.make_async_copy(fac_hbm.at[:, me], raw_f.at[me], own_sem.at[CHUNKS])
     gate_copy = pltpu.make_async_copy(gate_hbm, gate, gate_sem)
 
     def remote(src, dst, ss, rs, device):
@@ -128,10 +128,10 @@
         )
 
     def fac_out(g):
-        return remote(fac_hbm.at[g], raw_f.at[me], fac_ss.at[g], fac_rs.at[me], owner(g))
+        return remote(fac_hbm.at[:, g], raw_f.at[me], fac_ss.at[g], fac_rs.at[me], owner(g))
 
     def fac_arrive(k):
-        return remote(fac_hbm.at[k], raw_f.at[k], fac_ss.at[k], fac_rs.at[k], owner(k))
+        return remote(fac_hbm.at[:, k], raw_f.at[k], fac_ss.at[k], fac_rs.at[k], owner(k))
 
     last_rows = pl.ds(SPAN - 16, 16)
 
@@ -141,7 +141,7 @@
         )
 
     tail_f_copy = remote(
-        raw_f.at[GROUPS - 1, :, last_rows], tail_f, tail_ss.at[CHUNKS], tail_rs.at[CHUNKS], following
+        raw_f.at[GROUPS - 1, last_rows], tail_f, tail_ss.at[CHUNKS], tail_rs.at[CHUNKS], following
     )
 
     def stp_out(g):
@@ -185,22 +185,37 @@
     def y_arrive(k, c):
         return remote(y_send.at[k, c], y_recv.at[k, c], y_ss.at[k, c], y_rs.at[k, c], owner(k))
 
+    small = [
+        pltpu.make_async_copy(source, target, small_sem.at[i])
+        for i, (source, target) in enumerate(
+            [
+                (step_hbm, step_in), (conv_v_hbm, conv_v), (conv_f_hbm, conv_f),
+                (decay_hbm, decay), (skip_hbm, skip), (gain_hbm, gain),
+            ]
+        )
+    ]
+    small[0].start()
     barrier = pltpu.get_barrier_semaphore()
 
     @pl.loop(1, GROUPS)
     def _(j):
         pl.semaphore_signal(barrier, inc=1, device_id=owner(other(j)), device_id_type=MESH)
 
-    @pl.loop(1, supers)
-    def _(j):
-        pl.semaphore_signal(barrier, inc=1, device_id=column(other_super(j)), device_id_type=MESH)
-
+    pairs = [1 << d for d in range(supers.bit_length() - 1)]
+
+    def opposite(pair):
+        return column(mine + pair - 2 * pair * lax.rem(mine // pair, 2))
+
+    for pair in pairs:
+        pl.semaphore_signal(barrier, inc=1, device_id=opposite(pair), device_id_type=MESH)
+
+    small[0].wait()
     for start in range(0, GROUPS * heads, 128):
         count = min(128, GROUPS * heads - start)
         turned = jnp.transpose(step_in[:, start : start + count].astype(F32)).astype(BF16)
         stp_send[start // heads : (start + count) // heads] = turned.reshape(count // heads, heads, SPAN)
 
-    pl.semaphore_wait(barrier, GROUPS - 1 + supers - 1)
+    pl.semaphore_wait(barrier, GROUPS - 1 + len(pairs))
 
     @pl.loop(1, GROUPS)
     def _(j):
@@ -217,6 +232,8 @@
             sig_out(other(j), c).start()
 
     own_factors.start()
+    for copy in small[1:]:
+        copy.start()
     for c in range(CHUNKS):
         own_copy(c).start()
     gate_copy.start()
@@ -231,6 +248,10 @@
             )
         return head_col[pl.ds(pl.multiple_of(me * heads, heads), heads), :]
 
+    for d, pair in enumerate(pairs):
+        pl.semaphore_signal(met.at[d], inc=1, device_id=opposite(pair), device_id_type=MESH)
+        pl.semaphore_wait(met.at[d], 1)
+
     slot = lax.broadcasted_iota(jnp.int32, (128, channels), 0)
     channel = lax.broadcasted_iota(jnp.int32, (128, channels), 1)
     hit = jnp.zeros((128, channels), F32)
@@ -243,10 +264,12 @@
             columns, expander[:, c * width + lb : c * width + lb + lanes], preferred_element_type=F32
         )
 
-    skip_columns = split_columns(turn_row(skip))
+    for copy in small[1:]:
+        copy.wait()
+    skip_columns = split_columns(turn_row(skip[...]))
     for lb in range(0, channels, lanes):
         skip_row[:, lb : lb + lanes] = expand(skip_columns[0:16, :], 0, lb)[0:8]
-    rate = jnp.exp(turn_row(decay))
+    rate = jnp.exp(turn_row(decay[...]))
 
     def tail_before(rows):
         return jnp.where(mine > 0, rows.astype(F32), 0.0)
@@ -262,7 +285,7 @@
     def factors_of(k, before):
         for part_index, target in ((0, b_rows), (1, c_rows)):
             taps = conv_f[:, me, part_index, :].astype(F32)
-            target[k] = convolved(raw_f[k, part_index].astype(F32), before(part_index), taps)
+            target[k] = convolved(raw_f[k, :, part_index, :].astype(F32), before(part_index), taps)
 
     @pl.loop(1, GROUPS)
     def _(j):
@@ -316,11 +339,11 @@
 
     @pl.loop(1, GROUPS)
     def _(k):
-        factors_of(k, lambda i: raw_f[k - 1, i, SPAN - 16 : SPAN, :].astype(F32)[8:16])
+        factors_of(k, lambda i: raw_f[k - 1, SPAN - 8 : SPAN, i, :].astype(F32))
         scores_of(k)
 
     tail_f_copy.wait_recv()
-    factors_of(0, lambda i: tail_before(tail_f[i])[8:16])
+    factors_of(0, lambda i: tail_before(tail_f[:, i, :])[8:16])
     scores_of(0)
 
     def wait_chunk(c):
@@ -462,7 +485,7 @@
 
         @pl.loop(0, GROUPS)
         def _(j):
-            k = other(j)
+            k = other(GROUPS - j)
 
             @pl.when(j > 0)
             def _():
@@ -531,6 +554,22 @@
         out_copy(other(j)).wait()
 
 
+def move(strips, source, target, held, in_sem, out_sem):
+    high = held.shape[0] // strips
+    reads, writes = [], []
+    for i in range(strips):
+        here = pl.ds(i * high, high)
+        reads.append(pltpu.make_async_copy(source.at[here], held.at[here], in_sem.at[i]))
+        writes.append(pltpu.make_async_copy(held.at[here], target.at[here], out_sem.at[i]))
+    for read in reads:
+        read.start()
+    for read, write in zip(reads, writes):
+        read.wait()
+        write.start()
+    for write in writes:
+        write.wait()
+
+
 def local(
     values_in, factors_in, step_raw, gate_in, conv_values, conv_factors, decay_log, skip_gain, norm_gain
 ):
@@ -541,19 +580,18 @@
     supers = lax.axis_size("seq") // 2
     slice_rows = STATE // supers
 
-    fac = jnp.transpose(factors_in, (1, 2, 0, 3))
     gain = norm_gain.reshape(GROUPS, 1, channels)
 
-    vmem = pl.BlockSpec(memory_space=pltpu.VMEM)
     hbm = pl.BlockSpec(memory_space=pl.ANY)
     dma = pltpu.SemaphoreType.DMA
-    scratch = [
+    small = [step_raw, conv_values, conv_factors, decay_log.reshape(1, -1), skip_gain.reshape(1, -1), gain]
+    scratch = [pltpu.VMEM(array.shape, array.dtype) for array in small] + [
         pltpu.VMEM((SPAN, inner), BF16),
         pltpu.VMEM((SPAN, inner), BF16),
         pltpu.VMEM((CHUNKS, 16, width), BF16),
-        pltpu.VMEM((2, 16, STATE), BF16),
+        pltpu.VMEM((16, 2, STATE), BF16),
         pltpu.VMEM((GROUPS, CHUNKS, SPAN, width), BF16),
-        pltpu.VMEM((GROUPS, 2, SPAN, STATE), BF16),
+        pltpu.VMEM((GROUPS, SPAN, 2, STATE), BF16),
         pltpu.VMEM((GROUPS, CHUNKS, SPAN, width), BF16),
         pltpu.VMEM((GROUPS, SPAN, STATE), BF16),
         pltpu.VMEM((GROUPS, SPAN, STATE), BF16),
@@ -592,11 +630,12 @@
         dma((CHUNKS, supers)), dma((CHUNKS, supers)),
         dma((CHUNKS, supers)), dma((CHUNKS, supers)),
         dma((GROUPS, CHUNKS)), dma((GROUPS, CHUNKS)),
+        pltpu.SemaphoreType.REGULAR((supers.bit_length() - 1,)), dma((6,)),
     ]
-    return pl.pallas_call(
+    mixed = pl.pallas_call(
         partial(body, heads=heads, supers=supers),
         out_shape=jax.ShapeDtypeStruct((rows, inner), BF16),
-        in_specs=[hbm, hbm, hbm] + [vmem] * 6,
+        in_specs=[hbm] * 9,
         out_specs=hbm,
         scratch_shapes=scratch,
         compiler_params=pltpu.CompilerParams(
@@ -604,9 +643,17 @@
         ),
         name="layer",
     )(
-        values_in, gate_in, fac, step_raw, conv_values, conv_factors,
-        decay_log.reshape(1, -1), skip_gain.reshape(1, -1), gain,
+        values_in, gate_in, factors_in, *small
     )
+    strips = 4
+    return pl.pallas_call(
+        partial(move, strips),
+        out_shape=jax.ShapeDtypeStruct((rows, inner), BF16),
+        in_specs=[hbm],
+        out_specs=hbm,
+        scratch_shapes=[pltpu.VMEM((rows, inner), BF16), dma((strips,)), dma((strips,))],
+        name="move",
+    )(mixed)
 
 
 def solution(mesh):

time: 127 us -> 119 us (0.937)
  local copies, waits for them, and re-layouts: 7.1 us -> 0 us
  Pallas kernels: 120 us -> 118 us
    unnamed x2 -> x0, local copies, waits for them, and re-layouts: 7.1 us -> none
    pallas_call x1, Pallas kernels: 120 us -> 115 us  [local(): pl.pallas_call(partial(body, heads=heads, supers=supers), out_shape=jax.S...]
    pallas_call x0 -> x1, Pallas kernels: none -> 3.3 us  [local(): pl.pallas_call(partial(move, strips), out_shape=jax.ShapeDtypeStruct((row...]
where the time goes in v3:
time: 119 us; the launch traced here: 118 us
  Pallas kernels  118 us (99%)
    pallas_call x1, Pallas kernels, local(): pl.pallas_call(partial(body, heads=heads, supers=supers), out_shape=jax.S...  115 us
    pallas_call x1, Pallas kernels, local(): pl.pallas_call(partial(move, strips), out_shape=jax.ShapeDtypeStruct((row...  3.3 us

profile of v3, /device:TPU:0, one launch (start us, length us, event | category | flops | bytes accessed | tf_op | source)
XLA Modules:
  0.0 118.5 jit_solution(17451523324426512302)
XLA Ops:
  0.0 115.2 %layer.1.source = bf16[128,16384]{1,0:T(8,128)(2,1)} custom-call(bf16[128,16384]{1,0:T(8,128)(2,1)} %values_hbm.1, bf16[128,16384]{1,0:T(8,128)(2,1)} %gate_hbm.1, bf16[128,8,2,256]{3,2,1,0:T(2,128)(2,1)} %fac_hbm.1, bf16[128,256]{1,0:T(8,128)(2,1)} %step_hbm.1, bf16[4,16384]{1,0:T(4,128)(2,1)} %conv_v_hbm.1, bf16[4,8,2,256]{3,2,1,0:T(2,128)(2,1)} %conv_f_hbm.1, ...), custom_call_target="tpu_custom_call" | custom-call | tf_op jit(solution)/shard_map/layer/pallas_call | solution.py:635
  115.2 3.3 %move.1 = bf16[128,16384]{1,0:T(8,128)(2,1)} custom-call(bf16[128,16384]{1,0:T(8,128)(2,1)} %layer.1.source), custom_call_target="tpu_custom_call" | custom-call | tf_op jit(solution)/shard_map/move/pallas_call | solution.py:649

commit v4 on v3

--- a/solution.py
+++ b/solution.py
@@ -67,7 +67,7 @@
     part, weighted, gated, squares, y_send, y_recv,
     own_sem, gate_sem, out_sem, tail_ss, tail_rs,
     sig_ss, sig_rs, fac_ss, fac_rs, stp_ss, stp_rs, d_ss, d_rs,
-    st_ss, st_rs, e_ss, e_rs, y_ss, y_rs, met, small_sem,
+    st_ss, st_rs, e_ss, e_rs, y_ss, y_rs, met, all_met, small_sem,
     *, heads, supers,
 ):
     channels = heads * HEAD_DIM
@@ -206,8 +206,10 @@
     def opposite(pair):
         return column(mine + pair - 2 * pair * lax.rem(mine // pair, 2))
 
-    for pair in pairs:
-        pl.semaphore_signal(barrier, inc=1, device_id=opposite(pair), device_id_type=MESH)
+    @pl.when(me == 0)
+    def _():
+        for pair in pairs:
+            pl.semaphore_signal(barrier, inc=1, device_id=opposite(pair), device_id_type=MESH)
 
     small[0].wait()
     for start in range(0, GROUPS * heads, 128):
@@ -215,7 +217,7 @@
         turned = jnp.transpose(step_in[:, start : start + count].astype(F32)).astype(BF16)
         stp_send[start // heads : (start + count) // heads] = turned.reshape(count // heads, heads, SPAN)
 
-    pl.semaphore_wait(barrier, GROUPS - 1 + len(pairs))
+    pl.semaphore_wait(barrier, GROUPS - 1 + jnp.where(me == 0, len(pairs), 0))
 
     @pl.loop(1, GROUPS)
     def _(j):
@@ -248,9 +250,15 @@
             )
         return head_col[pl.ds(pl.multiple_of(me * heads, heads), heads), :]
 
-    for d, pair in enumerate(pairs):
-        pl.semaphore_signal(met.at[d], inc=1, device_id=opposite(pair), device_id_type=MESH)
-        pl.semaphore_wait(met.at[d], 1)
+    @pl.when(me == 0)
+    def _():
+        for d, pair in enumerate(pairs):
+            pl.semaphore_signal(met.at[d], inc=1, device_id=opposite(pair), device_id_type=MESH)
+            pl.semaphore_wait(met.at[d], 1)
+
+        @pl.loop(1, GROUPS)
+        def _(j):
+            pl.semaphore_signal(all_met, inc=1, device_id=owner(other(j)), device_id_type=MESH)
 
     slot = lax.broadcasted_iota(jnp.int32, (128, channels), 0)
     channel = lax.broadcasted_iota(jnp.int32, (128, channels), 1)
@@ -314,6 +322,10 @@
         return prior + ending
 
     lax.fori_loop(0, GROUPS, columns_of, jnp.zeros((heads, 1), F32))
+
+    @pl.when(me != 0)
+    def _():
+        pl.semaphore_wait(all_met, 1)
 
     @pl.loop(1, supers)
     def _(j):
@@ -630,7 +642,7 @@
         dma((CHUNKS, supers)), dma((CHUNKS, supers)),
         dma((CHUNKS, supers)), dma((CHUNKS, supers)),
         dma((GROUPS, CHUNKS)), dma((GROUPS, CHUNKS)),
-        pltpu.SemaphoreType.REGULAR((supers.bit_length() - 1,)), dma((6,)),
+        pltpu.SemaphoreType.REGULAR((supers.bit_length() - 1,)), pltpu.SemaphoreType.REGULAR, dma((6,)),
     ]
     mixed = pl.pallas_call(
         partial(body, heads=heads, supers=supers),

time: 119 us -> 117 us (0.983)
    pallas_call x1, Pallas kernels: 115 us -> 114 us  [local(): pl.pallas_call(partial(body, heads=heads, supers=supers), out_shape=jax.S...]
where the time goes in v4:
time: 117 us
  Pallas kernels  117 us (100%)
    pallas_call x1, Pallas kernels, local(): pl.pallas_call(partial(body, heads=heads, supers=supers), out_shape=jax.S...  114 us
    pallas_call x1, Pallas kernels, local(): pl.pallas_call(partial(move, strips), out_shape=jax.ShapeDtypeStruct((row...  3.3 us

profile of v4, /device:TPU:0, one launch (start us, length us, event | category | flops | bytes accessed | tf_op | source)
XLA Modules:
  0.0 117.0 jit_solution(12388253825290353992)
XLA Ops:
  0.0 113.7 %layer.1.source = bf16[128,16384]{1,0:T(8,128)(2,1)} custom-call(bf16[128,16384]{1,0:T(8,128)(2,1)} %values_hbm.1, bf16[128,16384]{1,0:T(8,128)(2,1)} %gate_hbm.1, bf16[128,8,2,256]{3,2,1,0:T(2,128)(2,1)} %fac_hbm.1, bf16[128,256]{1,0:T(8,128)(2,1)} %step_hbm.1, bf16[4,16384]{1,0:T(4,128)(2,1)} %conv_v_hbm.1, bf16[4,8,2,256]{3,2,1,0:T(2,128)(2,1)} %conv_f_hbm.1, ...), custom_call_target="tpu_custom_call" | custom-call | tf_op jit(solution)/shard_map/layer/pallas_call | solution.py:647
  113.7 3.3 %move.1 = bf16[128,16384]{1,0:T(8,128)(2,1)} custom-call(bf16[128,16384]{1,0:T(8,128)(2,1)} %layer.1.source), custom_call_target="tpu_custom_call" | custom-call | tf_op jit(solution)/shard_map/move/pallas_call | solution.py:661

commit v5 on v4

--- a/solution.py
+++ b/solution.py
@@ -511,7 +511,8 @@
                 value = y_recv[k, c, :, lb : lb + lanes].astype(F32) * silu_wide(
                     gate[:, here].astype(F32)
                 )
-                gated[k, :, c * width + lb : c * width + lb + lanes] = value
+                there = slice(c * width + lb, c * width + lb + lanes)
+                gated[k, :, there] = value * gain[k, :, there]
                 square = value * value
                 for start in range(0, lanes, 128):
                     total = total + square[:, start : start + 128]
@@ -523,7 +524,7 @@
                 for lb in range(0, channels, LANES):
                     here = pl.ds(pl.multiple_of(k * channels + lb, LANES), LANES)
                     out[:, here] = (
-                        gated[k, :, lb : lb + LANES] * inverse * gain[k, :, lb : lb + LANES]
+                        gated[k, :, lb : lb + LANES] * inverse
                     ).astype(BF16)
                 out_copy(k).start()
 

time: 117 us -> 117 us (level)
  no operation moved by 1% of the time
where the time goes in v5:
time: 117 us
  Pallas kernels  117 us (100%)
    pallas_call x1, Pallas kernels, local(): pl.pallas_call(partial(body, heads=heads, supers=supers), out_shape=jax.S...  114 us
    pallas_call x1, Pallas kernels, local(): pl.pallas_call(partial(move, strips), out_shape=jax.ShapeDtypeStruct((row...  3.3 us

profile of v5, /device:TPU:0, one launch (start us, length us, event | category | flops | bytes accessed | tf_op | source)
XLA Modules:
  0.0 116.9 jit_solution(6125075219263861862)
XLA Ops:
  0.0 113.6 %layer.1.source = bf16[128,16384]{1,0:T(8,128)(2,1)} custom-call(bf16[128,16384]{1,0:T(8,128)(2,1)} %values_hbm.1, bf16[128,16384]{1,0:T(8,128)(2,1)} %gate_hbm.1, bf16[128,8,2,256]{3,2,1,0:T(2,128)(2,1)} %fac_hbm.1, bf16[128,256]{1,0:T(8,128)(2,1)} %step_hbm.1, bf16[4,16384]{1,0:T(4,128)(2,1)} %conv_v_hbm.1, bf16[4,8,2,256]{3,2,1,0:T(2,128)(2,1)} %conv_f_hbm.1, ...), custom_call_target="tpu_custom_call" | custom-call | tf_op jit(solution)/shard_map/layer/pallas_call | solution.py:648
  113.6 3.3 %move.1 = bf16[128,16384]{1,0:T(8,128)(2,1)} custom-call(bf16[128,16384]{1,0:T(8,128)(2,1)} %layer.1.source), custom_call_target="tpu_custom_call" | custom-call | tf_op jit(solution)/shard_map/move/pallas_call | solution.py:662
